TPU v7x, 256 devices: a whole 4x4x8 slice. The times are simulated.
256 devices in a mesh: occ: 8 (over z_lo, y), aux: 32 (over x, z_hi, core).
Axes of the slice: x: 4, y: 4, z: 8 (z_hi: 4, z_lo: 2; z = z_hi * 2 + z_lo), core: 2. Of those that a mesh axis runs over, the one named last changes fastest.
Arguments:
- b_factors: bfloat16 [10752, 16, 2048], P('aux', 'occ'), may hold values from -0.25 to 0.25
- occ_energy: float32 [16], replicated, may hold values from -1.2 to -0.3
- vir_energy: float32 [2048], replicated, may hold values from 0.3 to 4
- slab_owner: int32 [32], replicated, may hold values from 0 to 31, each once
- pair_mask: int32 [8, 3, 32], P('occ'), may hold values from 0 to 1, as said below
Outputs:
- gamma: bfloat16 [10752, 16, 2048], P('aux', 'occ')
Inputs may be any that keep to these rules, and one draw needn't show every extreme that they name: pair_mask[I, 1, s] is 1 everywhere; pair_mask[I, 0, s] equals pair_mask[I', 2, s] where I' is the block before I (cyclically).
All inputs are finite; a program needn't handle non-finite values.
Results may differ from a plain program's by a relative error of at most 0.0047.
Values may be sent and summed in bfloat16 or wider, within the bound.
A program may use at most 128 MiB of HBM per device.

v0:
```python
import jax
import jax.numpy as jnp
from jax import lax
from jax.sharding import PartitionSpec as P

SLAB = 64


def passed_along(block, axis, distance):
    devices = range(lax.axis_size(axis))
    route = [((i - distance) % len(devices), i) for i in devices]
    return lax.ppermute(block, axis, route)


def pair_terms(own_panel, partner_panel, eps_own, eps_partner, eps_slab, weight):
    coulomb = jnp.einsum(
        "pisa,pjsb->sijab", own_panel, partner_panel, preferred_element_type=jnp.float32
    )
    denominator = (
        eps_slab[:, None, None, :, None]
        + eps_slab[:, None, None, None, :]
        - eps_own[None, :, None, None, None]
        - eps_partner[None, None, :, None, None]
    )
    amplitude = (2.0 * coulomb - jnp.swapaxes(coulomb, 3, 4)) / denominator
    amplitude = (amplitude * weight[:, None, None, None, None]).astype(jnp.bfloat16)
    return jnp.einsum(
        "sijab,pjsb->pisa", amplitude, partner_panel, preferred_element_type=jnp.float32
    )


def offset_term(own_panel, partner_panel, eps_own, eps_partner, eps_slab, weight):
    return pair_terms(own_panel, partner_panel, eps_own, eps_partner, eps_slab, weight)


def on_device(b_factors, occ_energy, vir_energy, slab_owner, pair_mask):
    aux_rows, occ_rows, virtuals = b_factors.shape
    slab_count = virtuals // SLAB
    slab_share = slab_count // lax.axis_size("aux")
    aux_rank = lax.axis_index("aux")
    occ_rank = lax.axis_index("occ")
    owned_slabs = lax.dynamic_slice_in_dim(slab_owner, aux_rank * slab_share, slab_share)
    onehot = (owned_slabs[:, None] == jnp.arange(slab_count, dtype=jnp.int32)[None, :]).astype(
        jnp.float32
    )
    eps_slab = jnp.dot(
        onehot, vir_energy.reshape(slab_count, SLAB), precision=lax.Precision.HIGHEST
    )
    active = jnp.dot(pair_mask[0].astype(jnp.float32), onehot.T, precision=lax.Precision.HIGHEST)
    eps_blocks = occ_energy.reshape(-1, occ_rows)
    block_count = eps_blocks.shape[0]

    def block_eps(offset):
        return lax.dynamic_index_in_dim(
            eps_blocks, (occ_rank + offset) % block_count, 0, keepdims=False
        )

    local_panel = b_factors.reshape(aux_rows, occ_rows, slab_count, SLAB)
    ordered = jnp.take(local_panel, slab_owner, axis=2)
    raw_panels = [passed_along(ordered, "occ", -offset) for offset in (-1, 1)]
    own_panel, lower_panel, upper_panel = (
        lax.all_to_all(ordered, "aux", split_axis=2, concat_axis=0, tiled=True),
        lax.all_to_all(raw_panels[0], "aux", split_axis=2, concat_axis=0, tiled=True),
        lax.all_to_all(raw_panels[1], "aux", split_axis=2, concat_axis=0, tiled=True),
    )
    eps_own = block_eps(0)
    gamma_sum = offset_term(own_panel, own_panel, eps_own, eps_own, eps_slab, active[1])
    gamma_sum = gamma_sum + offset_term(
        own_panel, lower_panel, eps_own, block_eps(-1), eps_slab, active[0]
    )
    gamma_sum = gamma_sum + offset_term(
        own_panel, upper_panel, eps_own, block_eps(1), eps_slab, active[2]
    )
    returned = lax.all_to_all(
        gamma_sum.astype(jnp.bfloat16), "aux", split_axis=0, concat_axis=2, tiled=True
    )
    return returned.reshape(aux_rows, occ_rows, virtuals)


def solution(mesh):
    placed = (P("aux", "occ", None), P(), P(), P(), P("occ", None, None))
    return jax.shard_map(
        on_device, mesh=mesh, in_specs=placed, out_specs=P("aux", "occ", None), check_vma=False
    )
```

profile of v0, /device:TPU:33, one launch (start us, length us, event | category | flops | bytes accessed | tf_op | source)
XLA Modules:
  0.0 541.3 jit_solution(1790036806153731414)
XLA Ops:
  0.0 0.7 compare_and_fusion
  0.7 0.7 compare_select_fusion
  1.3 8.7 %copy.30 = bf16[336,2,2048]{0,2,1:T(8,128)(2,1)} copy(bf16[336,2,2048]{2,1,0:T(2,128)(2,1)} %param.5) | data formatting | bytes 5505024 | tf_op args[0]
  10.0 3.1 gather_fusion
  13.1 2.1 select_bitcast_fusion
  15.2 10.9 %all-to-all-start = ((bf16[336,2,32,64]{0,3,1,2:T(8,128)(2,1)}), bf16[336,2,32,64]{0,3,1,2:T(8,128)(2,1)S(1)}, u32[]{:S(2)}, u32[]{:S(2)}) async-start(bf16[336,2,32,64]{0,3,1,2:T(8,128)(2,1)} %select_bitcast_fusion), calls=%async_computation | async-start | bytes 6291456 | tf_op jit(solution)/shard_map/all_to_all | solution.py:62
  26.0 3.3 collective-permute-start.1
  29.3 132.0 %collective-permute-done.1 = bf16[336,2,32,64]{0,3,1,2:T(8,128)(2,1)} collective-permute-done((bf16[336,2,32,64]{0,3,1,2:T(8,128)(2,1)}, bf16[336,2,32,64]{0,3,1,2:T(8,128)(2,1)}, u32[]{:S(2)}, u32[]{:S(2)}) %collective-permute-start.1) | collective-permute-done | bytes 2752544 | tf_op jit(solution)/shard_map/ppermute | solution.py:12
  161.3 0.0 all-to-all-done
  161.3 0.0 copy-start
  161.3 9.7 %all-to-all-start.2 = ((bf16[336,2,32,64]{0,3,1,2:T(8,128)(2,1)}), bf16[336,2,32,64]{0,3,1,2:T(8,128)(2,1)}, u32[]{:S(2)}, u32[]{:S(2)}) async-start(bf16[336,2,32,64]{0,3,1,2:T(8,128)(2,1)} %collective-permute-done.1), calls=%async_computation.2 | async-start | bytes 6291456 | tf_op jit(solution)/shard_map/all_to_all | solution.py:64
  171.0 0.0 copy-start.5
  171.0 0.0 copy-start.3
  171.0 0.0 copy-start.4
  171.1 0.0 copy-start.2
  171.1 0.1 collective-permute-start
  171.2 140.3 %collective-permute-done = bf16[336,2,32,64]{0,3,1,2:T(8,128)(2,1)} collective-permute-done((bf16[336,2,32,64]{0,3,1,2:T(8,128)(2,1)}, bf16[336,2,32,64]{0,3,1,2:T(8,128)(2,1)}, u32[]{:S(2)}, u32[]{:S(2)}) %collective-permute-start) | collective-permute-done | bytes 2752544 | tf_op jit(solution)/shard_map/ppermute | solution.py:12
  311.5 0.0 all-to-all-done.2
  311.5 9.5 %all-to-all-start.1 = ((bf16[336,2,32,64]{0,3,1,2:T(8,128)(2,1)}), bf16[336,2,32,64]{0,3,1,2:T(8,128)(2,1)}, u32[]{:S(2)}, u32[]{:S(2)}) async-start(bf16[336,2,32,64]{0,3,1,2:T(8,128)(2,1)} %collective-permute-done), calls=%async_computation.1 | async-start | bytes 6291456 | tf_op jit(solution)/shard_map/all_to_all | solution.py:63
  321.0 0.0 copy-done.5
  321.0 0.6 dynamic_slice.13
  321.6 0.0 copy-done.3
  321.6 0.0 copy-done.4
  321.6 0.1 reshape.192
  321.7 0.0 copy-done.2
  321.7 0.1 reshape.191
  321.8 0.8 convolution_bitcast_fusion.4
  322.6 0.1 broadcast_add_fusion
  322.6 0.1 broadcast_subtract_fusion
  322.7 0.1 copy.61
  322.8 0.8 convolution_bitcast_fusion.3
  323.6 0.7 fusion.58
  324.3 1.6 fusion.8
  325.9 0.8 copy.33
  326.7 0.4 copy.93
  327.0 3.5 copy.32
  330.5 0.0 copy-start.1
  330.5 6.9 %reshape.216 = bf16[10752,2,64,1]{0,2,1,3:T(8,128)(2,1)} reshape(bf16[32,336,2,1,64]{1,0,4,2,3:T(8,128)(2,1)} %copy.32) | data formatting | bytes 5505024 | tf_op jit(solution)/shard_map/reshape.28
  337.5 0.0 copy-done.1
  337.5 5.9 %convolution_bitcast_fusion.2 = f32[10752,2,64]{0,2,1:T(8,128)} fusion(bf16[10752,2,64,1]{0,2,1,3:T(8,128)(2,1)} %reshape.216, f32[1,2,2,64,64]{4,3,1,2,0:T(8,128)S(1)} %copy-done.1, f32[2,64,2,64,1]{3,1,4,2,0:T(8,128)S(1)} %fusion.8, f32[]{:T(128)} %bitcast.20, f32[2]{0:T(128)S(1)} %get-tuple-element.7, f32[2,64,64]{2,1,0:T(8,128)S(1)} %broadcast_subtract_fusion), kind=kOutput, calls=%fused_computation.3 | convolution fusion | flops 352403456 | bytes 8421388 | tf_op jit(solution)/shard_map/sijab,pjsb->pisa/dot_general | solution.py:27
  343.4 2.3 copy.91
  345.6 3.5 copy.42
  349.1 6.9 %reshape.224 = bf16[10752,2,64,1]{0,2,1,3:T(8,128)(2,1)} reshape(bf16[32,336,2,1,64]{1,0,4,2,3:T(8,128)(2,1)} %copy.42) | data formatting | bytes 5505024 | tf_op jit(solution)/shard_map/reshape.58
  356.0 0.0 copy-done
  356.0 3.5 fusion.4
  359.6 0.1 copy.43
  359.7 35.7 %all-to-all-done.1 = bf16[336,2,32,64]{0,3,1,2:T(8,128)(2,1)} async-done(((bf16[336,2,32,64]{0,3,1,2:T(8,128)(2,1)}), bf16[336,2,32,64]{0,3,1,2:T(8,128)(2,1)}, u32[]{:S(2)}, u32[]{:S(2)}) %all-to-all-start.1) | async-done | bytes 2752544 | tf_op jit(solution)/shard_map/all_to_all | solution.py:63
  395.3 2.3 copy.92
  397.6 3.5 copy.36
  401.1 5.9 %reshape.220 = bf16[10752,2,64,1]{0,2,1,3:T(8,128)(2,1)S(1)} reshape(bf16[32,336,2,1,64]{1,0,4,2,3:T(8,128)(2,1)} %copy.36) | data formatting | bytes 5505024 | tf_op jit(solution)/shard_map/reshape.44
  407.0 4.4 fusion.6
  411.4 0.1 copy.38
  411.5 0.0 slice-start
  411.5 0.0 slice-start.1
  411.6 3.9 convolution_bitcast_fusion
  415.5 0.0 slice-done
  415.5 0.0 slice-done.1
  415.5 3.2 fusion.3
  418.7 12.1 %copy.45 = bf16[10752,2,1,64]{3,1,2,0:T(2,128)(2,1)} copy(bf16[10752,2,1,64]{0,3,1,2:T(8,128)(2,1)} %fusion.3) | data formatting | bytes 5505024 | tf_op jit(solution)/shard_map/convert_element_type | solution.py:75
  430.8 11.5 %reshape.229 = bf16[32,2,21504]{2,1,0:T(2,128)(2,1)S(1)} reshape(bf16[10752,1,2,64]{3,2,1,0:T(2,128)(2,1)} %bitcast.194) | data formatting | bytes 5505024
  442.3 71.2 %all_to_all.60 = bf16[32,2,21504]{2,1,0:T(2,128)(2,1)} all-to-all(bf16[32,2,21504]{2,1,0:T(2,128)(2,1)S(1)} %reshape.229), channel_id=1, replica_groups=mesh['occ'=8,'aux'=32] {'aux'}, dimensions={0} | all-to-all | bytes 5505024 | tf_op jit(solution)/shard_map/all_to_all | solution.py:74
  513.5 12.3 %reshape.230 = bf16[10752,1,2,64]{3,2,1,0:T(2,128)(2,1)} reshape(bf16[32,2,21504]{2,1,0:T(2,128)(2,1)} %all_to_all.60) | data formatting | bytes 5505024
  525.8 9.8 %copy.46 = bf16[32,336,2,1,64]{1,4,0,2,3:T(8,128)(2,1)S(1)} copy(bf16[32,336,2,1,64]{4,2,1,0,3:T(2,128)(2,1)} %bitcast.195) | data formatting | bytes 5505024 | tf_op jit(solution)/shard_map/all_to_all | solution.py:74
  535.6 5.7 %copy.47 = bf16[336,2,2048]{2,1,0:T(2,128)(2,1)} copy(bf16[336,2,2048]{0,2,1:T(8,128)(2,1)S(1)} %bitcast.196) | data formatting | bytes 5505024 | tf_op jit(solution)/shard_map/reshape | solution.py:77
  (6 shorter events, 0.0 us)
Async XLA Ops:
  15.2 146.2 %all-to-all-start = ((bf16[336,2,32,64]{0,3,1,2:T(8,128)(2,1)}), bf16[336,2,32,64]{0,3,1,2:T(8,128)(2,1)S(1)}, u32[]{:S(2)}, u32[]{:S(2)}) async-start(bf16[336,2,32,64]{0,3,1,2:T(8,128)(2,1)} %select_bitcast_fusion), calls=%async_computation | async-start | bytes 6291456 | tf_op jit(solution)/shard_map/all_to_all | solution.py:62
  26.0 135.3 %collective-permute-start.1 = (bf16[336,2,32,64]{0,3,1,2:T(8,128)(2,1)}, bf16[336,2,32,64]{0,3,1,2:T(8,128)(2,1)}, u32[]{:S(2)}, u32[]{:S(2)}) collective-permute-start(bf16[336,2,32,64]{0,3,1,2:T(8,128)(2,1)} %select_bitcast_fusion), channel_id=1, source_target_pairs={{32,0},{64,32},{96,64},{128,96},{160,128},{192,160},{224,192},{0,2... | collective-permute-start | bytes 8257544 | tf_op jit(solution)/shard_map/ppermute | solution.py:12
  161.3 194.7 %copy-start = (bf16[336,2,32,64]{0,3,1,2:T(8,128)(2,1)}, bf16[336,2,32,64]{0,3,1,2:T(8,128)(2,1)S(1)}, u32[]{:S(2)}) copy-start(bf16[336,2,32,64]{0,3,1,2:T(8,128)(2,1)S(1)} %all-to-all-done) | copy-start | bytes 8257540
  161.3 150.2 %all-to-all-start.2 = ((bf16[336,2,32,64]{0,3,1,2:T(8,128)(2,1)}), bf16[336,2,32,64]{0,3,1,2:T(8,128)(2,1)}, u32[]{:S(2)}, u32[]{:S(2)}) async-start(bf16[336,2,32,64]{0,3,1,2:T(8,128)(2,1)} %collective-permute-done.1), calls=%async_computation.2 | async-start | bytes 6291456 | tf_op jit(solution)/shard_map/all_to_all | solution.py:64
  171.0 150.0 %copy-start.5 = (s32[32]{0:T(128)S(1)}, s32[32]{0:T(128)}, u32[]{:S(2)}) copy-start(s32[32]{0:T(128)} %param.8) | copy-start | bytes 388
  171.0 150.6 %copy-start.3 = (s32[1,3,32]{2,0,1:T(1,128)S(1)}, s32[1,3,32]{2,0,1:T(1,128)}, u32[]{:S(2)}) copy-start(s32[1,3,32]{2,0,1:T(1,128)} %param.9) | copy-start | bytes 1156
  171.0 150.6 %copy-start.4 = (f32[16]{0:T(128)S(1)}, f32[16]{0:T(128)}, u32[]{:S(2)}) copy-start(f32[16]{0:T(128)} %param.6) | copy-start | bytes 196
  171.1 150.7 %copy-start.2 = (f32[2048]{0:T(1024)S(1)}, f32[2048]{0:T(1024)}, u32[]{:S(2)}) copy-start(f32[2048]{0:T(1024)} %param.7) | copy-start | bytes 24580
  171.1 140.4 %collective-permute-start = (bf16[336,2,32,64]{0,3,1,2:T(8,128)(2,1)}, bf16[336,2,32,64]{0,3,1,2:T(8,128)(2,1)}, u32[]{:S(2)}, u32[]{:S(2)}) collective-permute-start(bf16[336,2,32,64]{0,3,1,2:T(8,128)(2,1)} %select_bitcast_fusion), channel_id=1, source_target_pairs={{224,0},{0,32},{32,64},{64,96},{96,128},{128,160},{160,192},{192,2... | collective-permute-start | bytes 8257544 | tf_op jit(solution)/shard_map/ppermute | solution.py:12
  311.5 83.8 %all-to-all-start.1 = ((bf16[336,2,32,64]{0,3,1,2:T(8,128)(2,1)}), bf16[336,2,32,64]{0,3,1,2:T(8,128)(2,1)}, u32[]{:S(2)}, u32[]{:S(2)}) async-start(bf16[336,2,32,64]{0,3,1,2:T(8,128)(2,1)} %collective-permute-done), calls=%async_computation.1 | async-start | bytes 6291456 | tf_op jit(solution)/shard_map/all_to_all | solution.py:63
  330.5 6.9 %copy-start.1 = (f32[1,2,2,64,64]{4,3,1,2,0:T(8,128)S(1)}, f32[1,2,2,64,64]{4,3,1,2,0:T(8,128)}, u32[]{:S(2)}) copy-start(f32[1,2,2,64,64]{4,3,1,2,0:T(8,128)} %copy.33) | copy-start | bytes 196612
  411.5 4.0 slice-start
  411.5 4.0 slice-start.1
where the time goes:
time: 543 us; the launch traced here: 541 us
  waiting for transfers between devices  308 us (57%)
  local copies, waits for them, and re-layouts  101 us (19%)
  blocking collectives  71.2 us (13%)
  starting transfers between devices  33.3 us (6%)
  matrix products  24 us (4%)
    ppermute x2, waiting for transfers between devices, passed_along(): return lax.ppermute(block, axis, route)  272 us
    all_to_all x1, blocking collectives, on_device(): lax.all_to_all(gamma_sum.astype(jnp.bfloat16), 'aux', split_axis=0, conca...  71.2 us
    all_to_all x1, waiting for transfers between devices, on_device(): lax.all_to_all(raw_panels[0], 'aux', split_axis=2, concat_axis=0, tiled=T...  35.7 us
    unnamed x20, local copies, waits for them, and re-layouts  32.6 us
    another operation x3, local copies, waits for them, and re-layouts  19.7 us
    dot_general x3, matrix products, pair_terms(): jnp.einsum('sijab,pjsb->pisa', amplitude, partner_panel, preferred_elemen...  13 us
    convert_element_type x1, local copies, waits for them, and re-layouts, on_device(): gamma_sum.astype(jnp.bfloat16)  12.1 us
  transfers between devices with their start and end apart: 5, of which 3 were waited for; matrix products, arithmetic and copies ran while one was open for 7% of the time, Pallas kernels for 0%

commit v1 on v0

v1 whole, which is shorter than its diff:
```python
import functools

import jax
import jax.numpy as jnp
from jax import lax
from jax.experimental import pallas as pl
from jax.experimental.pallas import tpu as pltpu
from jax.sharding import PartitionSpec as P

SLAB = 64
LANES = 128
X, ZH, CORES = 4, 4, 2
HALF = 16
CHUNK = 4
PART = jnp.bfloat16
MESH = pl.DeviceIdType.MESH
VMEM = pltpu.VMEM


def low_half(shape):
    return lax.broadcasted_iota(jnp.int32, shape, len(shape) - 1) < SLAB


def regroup_kernel(slab_ref, raw_ref, out_ref, wide):
    rows = out_ref.shape[1]
    step = 512

    @pl.loop(0, raw_ref.shape[0] // step)
    def _(n):
        at = pl.ds(pl.multiple_of(n * step, step), step)
        wide[at, :] = raw_ref[at, :].astype(jnp.float32)

    @pl.loop(0, out_ref.shape[0])
    def _(k):
        slab = slab_ref[k]
        tile = slab // 2
        odd = (slab % 2) == 1
        first = wide[pl.ds(tile * 2, rows, stride=32), :]
        second = wide[pl.ds(tile * 2 + 1, rows, stride=32), :]
        left = low_half(first.shape)
        in_order = jnp.where(left, first, pltpu.roll(second, SLAB, 1))
        swapped = jnp.where(left, pltpu.roll(first, SLAB, 1), second)
        out_ref[k] = jnp.where(odd, swapped, in_order).astype(out_ref.dtype)


def regroup(raw, slab_owner, rows, slabs):
    return pl.pallas_call(
        regroup_kernel,
        out_shape=jax.ShapeDtypeStruct((slabs, rows, LANES), raw.dtype),
        in_specs=[pl.BlockSpec(memory_space=pltpu.SMEM), pl.BlockSpec(memory_space=VMEM)],
        out_specs=pl.BlockSpec(memory_space=VMEM),
        scratch_shapes=[VMEM(raw.shape, jnp.float32)],
        compiler_params=pltpu.CompilerParams(vmem_limit_bytes=40 << 20),
        name="regroup",
    )(slab_owner, raw)


def ungroup_kernel(gamma_ref, raw_ref, wide):
    rows = gamma_ref.shape[1]
    step = 512

    @pl.loop(0, gamma_ref.shape[0] // 2)
    def _(tile):
        even = gamma_ref[2 * tile].astype(jnp.float32)
        odd = gamma_ref[2 * tile + 1].astype(jnp.float32)
        left = low_half(even.shape)
        wide[pl.ds(tile * 2, rows, stride=32), :] = jnp.where(left, even, pltpu.roll(odd, SLAB, 1))
        wide[pl.ds(tile * 2 + 1, rows, stride=32), :] = jnp.where(
            left, pltpu.roll(even, SLAB, 1), odd
        )

    @pl.loop(0, raw_ref.shape[0] // step)
    def _(n):
        at = pl.ds(pl.multiple_of(n * step, step), step)
        raw_ref[at, :] = wide[at, :].astype(raw_ref.dtype)


def ungroup(gamma):
    slabs, rows, _ = gamma.shape
    shape = (slabs * rows, LANES)
    return pl.pallas_call(
        ungroup_kernel,
        out_shape=jax.ShapeDtypeStruct(shape, gamma.dtype),
        in_specs=[pl.BlockSpec(memory_space=VMEM)],
        out_specs=pl.BlockSpec(memory_space=VMEM),
        scratch_shapes=[VMEM(shape, jnp.float32)],
        compiler_params=pltpu.CompilerParams(vmem_limit_bytes=40 << 20),
        name="ungroup",
    )(gamma)


def dot(a, b, ca, cb):
    return lax.dot_general(a, b, (((ca,), (cb,)), ((), ())), preferred_element_type=jnp.float32)


def density_kernel(
    occ_count,
    slab_ref, occ_ref, mask_ref, vir_ref, own_ref,
    out_ref,
    panel, near, part, part_wide, part_in, total, lower_out, lower_in,
    unit_out, unit_in, amp, gamma_out,
    copy_sem, core_send, core_recv, halo_send, halo_recv, x_send, x_recv, y_send, y_recv,
    z_send, z_recv, low_send, low_recv, za_send, za_recv, zl_send, zl_recv,
    xa_send, xa_recv, out_send, out_recv,
):
    o = lax.axis_index("occ")
    aux = lax.axis_index("aux")
    core = aux % CORES
    zh = (aux // CORES) % ZH
    x = aux // (CORES * ZH)
    other = 1 - core

    def device(occ, x_at, z_at, core_at):
        return (occ, (x_at * ZH + z_at) * CORES + core_at)

    below = lax.rem(o + occ_count - 1, occ_count)
    above = lax.rem(o + 1, occ_count)
    x_peers = [lax.rem(x + d, X) for d in range(X)]
    z_peers = [lax.rem(zh + d, ZH) for d in range(ZH)]
    my_half, my_row = zh // 2, zh % 2

    def remote(src, dst, send, recv, to):
        return pltpu.make_async_remote_copy(
            src_ref=src, dst_ref=dst, send_sem=send, recv_sem=recv, device_id=to,
            device_id_type=MESH,
        )

    partners = [device(o, x, zh, other)]
    partners += [device(b, x, zh, c) for b in (below, above) for c in (0, 1)]
    partners += [device(o, x_peers[d], zh, core) for d in range(1, X)]
    partners += [device(o, x, z_peers[d], core) for d in range(1, ZH)]
    barrier = pltpu.get_barrier_semaphore()
    for partner in partners:
        pl.semaphore_signal(barrier, inc=1, device_id=partner, device_id_type=MESH)
    pl.semaphore_wait(barrier, len(partners))

    chunks = HALF // CHUNK

    def slabs_of(core_at, j):
        return own_ref.at[pl.ds(core_at * HALF + j * CHUNK, CHUNK)]

    def core_copy(j):
        return remote(
            slabs_of(other, j), panel.at[core, pl.ds(j * CHUNK, CHUNK)],
            core_send.at[j], core_recv.at[j], device(o, x, zh, other),
        )

    def halo_copy(n, core_at):
        phase, j = divmod(n, chunks)
        way = core if phase == 0 else other
        to = jnp.where(way == 0, below, above)
        return remote(
            slabs_of(core_at, j), near.at[way, core, pl.ds(j * CHUNK, CHUNK)],
            halo_send.at[n, core_at], halo_recv.at[n, way], device(to, x, zh, core_at),
        )

    def halo_start(n):
        for core_at in (0, 1):
            halo_copy(n, core_at).start()

    def halo_wait_send(n):
        for core_at in (0, 1):
            halo_copy(n, core_at).wait_send()

    def halo_wait_recv(n):
        phase, j = divmod(n, chunks)
        for way in (0, 1):
            source_core = way if phase == 0 else 1 - way
            landed = near.at[way, source_core, pl.ds(j * CHUNK, CHUNK)]
            remote(landed, landed, halo_send.at[n, 0], halo_recv.at[n, way],
                   device(above, x, zh, source_core)).wait_recv()

    local = pltpu.make_async_copy(
        own_ref.at[pl.ds(core * HALF, HALF)], panel.at[core], copy_sem
    )
    halo_start(0)
    local.start()
    core_copy(0).start()
    halo_start(1)
    for j in range(1, chunks):
        core_copy(j).start()
    local.wait()

    def part_copy(g, h, d):
        to = x_peers[d]
        return remote(part.at[g, h, to], part_in.at[g, h, d], x_send.at[g, h, d],
                      x_recv.at[g, h, d], device(o, to, zh, core))

    def coulomb(j):
        g, h = divmod(j, 2)

        @pl.loop(0, CHUNK)
        def _(s):
            q = j * CHUNK + s
            first, second = panel[0, q], panel[1, q]
            sums = (
                dot(first, first, 0, 0) + dot(second, second, 0, 0),
                dot(first, near[0, 0, q], 0, 0),
                dot(near[1, 1, q], second, 0, 0),
            )
            for m in range(3):
                part_wide[g, h, s, m] = sums[m]
                part[g, h, s, m] = sums[m].astype(PART)

        for d in range(1, X):
            part_copy(g, h, d).start()

    def lower_copy(g):
        return remote(lower_out.at[g], lower_in.at[g], y_send.at[g], y_recv.at[g],
                      device(below, x, zh, core))

    def add_over_x(g):
        for h in range(2):
            for d in range(1, X):
                part_copy(g, h, d).wait_recv()
        for h in range(2):
            for m in range(3):
                value = part_wide[g, h, x, m]
                for d in range(1, X):
                    value = value + part_in[g, h, d, m].astype(jnp.float32)
                if m < 2:
                    total[g, h, m] = value
                else:
                    lower_out[g, h] = value.astype(PART)
        lower_copy(g).start()

    def unit_copy(g, d):
        to = z_peers[d]
        return remote(unit_out.at[g, to], unit_in.at[g, d], z_send.at[g, d], z_recv.at[g, d],
                      device(o, x, to, core))

    def spread_over_z(g):
        lower_copy(g).wait_recv()
        for h in range(2):
            total[g, h, 1] = total[g, h, 1] + lower_in[g, h].astype(jnp.float32)
            for m in range(2):
                for i in range(2):
                    unit_out[g, 2 * h + i, m] = total[g, h, m, i * SLAB : (i + 1) * SLAB].astype(PART)
        for d in range(1, ZH):
            unit_copy(g, d).start()

    def amp_copy(g, d):
        mine = amp.at[g, my_half, x, pl.ds(0, 2), my_row]
        return remote(mine, mine, za_send.at[g, d], za_recv.at[g, d], device(o, x, z_peers[d], core))

    def amp_up_copy(g):
        return remote(amp.at[g, my_half, x, 1, my_row], amp.at[g, my_half, x, 2, my_row],
                      low_send.at[g], low_recv.at[g], device(above, x, zh, core))

    def amp_low_copy(g, d):
        mine = amp.at[g, my_half, x, 2, my_row]
        return remote(mine, mine, zl_send.at[g, d], zl_recv.at[g, d], device(o, x, z_peers[d], core))

    def amplitude(g):
        for d in range(1, ZH):
            unit_copy(g, d).wait_recv()
        row = pl.multiple_of(my_row * SLAB, SLAB)
        halves = []
        for m in range(2):
            value = total[g, my_half, m, pl.ds(row, SLAB), :]
            for d in range(1, ZH):
                value = value + unit_in[g, d, m].astype(jnp.float32)
            halves.append(value)
        whole = jnp.concatenate(halves, axis=0)
        turned = whole.T
        crossed = pltpu.roll(
            jnp.concatenate([turned[SLAB:], turned[:SLAB]], axis=0), SLAB, 1
        )
        square = (LANES, LANES)
        left = low_half(square)
        top = lax.broadcasted_iota(jnp.int32, square, 0) < SLAB
        swapped = jnp.where(left == top, turned, crossed)
        k = core * HALF + g * 2 * CHUNK + my_half * CHUNK + x
        slab = slab_ref[k]
        line = vir_ref[pl.ds(slab // 2, 1), :]
        flipped = pltpu.roll(line, SLAB, 1)
        take = low_half(line.shape) == ((slab % 2) == 0)
        eps_b = jnp.broadcast_to(jnp.where(take, line, flipped), square)
        eps_i = occ_ref[2 * o + my_row]
        eps_j = jnp.where(
            top,
            jnp.where(left, occ_ref[2 * o], occ_ref[2 * o + 1]),
            jnp.where(left, occ_ref[2 * above], occ_ref[2 * above + 1]),
        )
        denominator = eps_b.T + eps_b - eps_i - eps_j
        weight = jnp.where(top, mask_ref[0, 1, slab], mask_ref[0, 2, slab]).astype(jnp.float32)
        value = ((2.0 * whole - swapped) / denominator * weight).astype(amp.dtype)
        amp[g, my_half, x, 0, my_row] = value[:SLAB]
        amp[g, my_half, x, 1, my_row] = value[SLAB:]
        amp_up_copy(g).start()
        for d in range(1, ZH):
            amp_copy(g, d).start()

    def pass_lower(g):
        amp_up_copy(g).wait_recv()
        for d in range(1, ZH):
            amp_low_copy(g, d).start()

    def from_z(g, d):
        peer = z_peers[ZH - d]
        return g, peer // 2, x, peer % 2

    def panel_copy(g, d):
        mine = amp.at[g, pl.ds(0, 2), x]
        return remote(mine, mine, xa_send.at[g, d], xa_recv.at[g, d],
                      device(o, x_peers[d], zh, core))

    def gather_over_x(g):
        for d in range(1, ZH):
            at, half, x_at, row = from_z(g, d)
            landed = amp.at[at, half, x_at, pl.ds(0, 2), row]
            remote(landed, landed, za_send.at[g, d], za_recv.at[g, d],
                   device(o, x, z_peers[d], core)).wait_recv()
            landed = amp.at[at, half, x_at, 2, row]
            remote(landed, landed, zl_send.at[g, d], zl_recv.at[g, d],
                   device(o, x, z_peers[d], core)).wait_recv()
        for d in range(1, X):
            panel_copy(g, d).start()

    def amps_here(g):
        for d in range(1, X):
            landed = amp.at[g, pl.ds(0, 2), x_peers[X - d]]
            remote(landed, landed, xa_send.at[g, d], xa_recv.at[g, d],
                   device(o, x_peers[d], zh, core)).wait_recv()

    def gamma_copy(j):
        return remote(
            gamma_out.at[pl.ds(j * CHUNK, CHUNK)],
            out_ref.at[pl.ds(core * HALF + j * CHUNK, CHUNK)],
            out_send.at[j], out_recv.at[j], device(o, x, zh, other),
        )

    def density(j):
        g, h = divmod(j, 2)

        @pl.loop(0, CHUNK)
        def _(s):
            q = j * CHUNK + s
            own, up, low = (
                amp[g, h, s, m].reshape(LANES, LANES) for m in range(3)
            )

            def rows(at):
                value = dot(panel[at, q], own, 1, 1) + dot(near[0, at, q], up, 1, 1)
                return (value + dot(near[1, at, q], low, 1, 0)).astype(out_ref.dtype)

            gamma_out[q] = rows(other)
            out_ref[core * HALF + q] = rows(core)

        gamma_copy(j).start()

    for j in range(chunks):
        core_copy(j).wait_recv()
        halo_wait_recv(j)
        halo_wait_send(j)
        halo_start(j + 2)
        coulomb(j)
        if j == 2:
            add_over_x(0)
    spread_over_z(0)
    amplitude(0)
    pass_lower(0)
    add_over_x(1)
    halo_wait_send(4)
    halo_start(6)
    gather_over_x(0)
    spread_over_z(1)
    amplitude(1)
    halo_wait_send(5)
    halo_start(7)
    pass_lower(1)
    gather_over_x(1)
    amps_here(0)
    for j in range(chunks):
        if j == 2:
            amps_here(1)
        halo_wait_recv(chunks + j)
        density(j)

    for n in (6, 7):
        halo_wait_send(n)
    for j in range(chunks):
        core_copy(j).wait_send()
    for g in range(2):
        for h in range(2):
            for d in range(1, X):
                part_copy(g, h, d).wait_send()
        lower_copy(g).wait_send()
        amp_up_copy(g).wait_send()
        for d in range(1, ZH):
            unit_copy(g, d).wait_send()
            amp_copy(g, d).wait_send()
            amp_low_copy(g, d).wait_send()
        for d in range(1, X):
            panel_copy(g, d).wait_send()
    for j in range(chunks):
        gamma_copy(j).wait_send()
        landed = out_ref.at[pl.ds(other * HALF + j * CHUNK, CHUNK)]
        remote(landed, landed, out_send.at[j], out_recv.at[j],
               device(o, x, zh, other)).wait_recv()


def density(grouped, slab_owner, occ_energy, pair_mask, vir_energy):
    slabs, rows, _ = grouped.shape
    dma = pltpu.SemaphoreType.DMA
    bf16, f32 = jnp.bfloat16, jnp.float32
    smem, vmem = pl.BlockSpec(memory_space=pltpu.SMEM), pl.BlockSpec(memory_space=VMEM)
    halos = 2 * HALF // CHUNK
    return pl.pallas_call(
        functools.partial(density_kernel, lax.axis_size("occ")),
        out_shape=jax.ShapeDtypeStruct(grouped.shape, bf16),
        in_specs=[smem, smem, smem, vmem, vmem],
        out_specs=vmem,
        scratch_shapes=[
            VMEM((2, HALF, rows, LANES), bf16),
            VMEM((2, 2, HALF, rows, LANES), bf16),
            VMEM((2, 2, X, 3, LANES, LANES), PART),
            VMEM((2, 2, X, 3, LANES, LANES), f32),
            VMEM((2, 2, X, 3, LANES, LANES), PART),
            VMEM((2, 2, 2, LANES, LANES), f32),
            VMEM((2, 2, LANES, LANES), PART),
            VMEM((2, 2, LANES, LANES), PART),
            VMEM((2, ZH, 2, SLAB, LANES), PART),
            VMEM((2, ZH, 2, SLAB, LANES), PART),
            VMEM((2, 2, X, 3, 2, SLAB, LANES), bf16),
            VMEM((HALF, rows, LANES), bf16),
            dma, dma((4,)), dma((4,)), dma((halos, 2)), dma((halos, 2)),
            dma((2, 2, X)), dma((2, 2, X)), dma((2,)), dma((2,)),
            dma((2, ZH)), dma((2, ZH)), dma((2,)), dma((2,)),
            dma((2, ZH)), dma((2, ZH)), dma((2, ZH)), dma((2, ZH)),
            dma((2, X)), dma((2, X)), dma((4,)), dma((4,)),
        ],
        compiler_params=pltpu.CompilerParams(
            collective_id=0, has_side_effects=True, vmem_limit_bytes=56 << 20
        ),
        name="density",
    )(slab_owner, occ_energy, pair_mask, vir_energy, grouped)


def on_device(b_factors, occ_energy, vir_energy, slab_owner, pair_mask):
    aux_rows, occ_rows, virtuals = b_factors.shape
    tiles = virtuals // LANES
    raw = b_factors.reshape(aux_rows, occ_rows, tiles, LANES)
    raw = jnp.swapaxes(raw, 1, 2).reshape(aux_rows * tiles * occ_rows, LANES)
    grouped = regroup(raw, slab_owner, aux_rows, virtuals // SLAB)
    gamma = density(
        grouped, slab_owner, occ_energy, pair_mask, vir_energy.reshape(tiles, LANES)
    )
    raw = ungroup(gamma).reshape(aux_rows, tiles, occ_rows, LANES)
    return jnp.swapaxes(raw, 1, 2).reshape(aux_rows, occ_rows, virtuals)


def solution(mesh):
    placed = (P("aux", "occ", None), P(), P(), P(), P("occ", None, None))
    return jax.shard_map(
        on_device, mesh=mesh, in_specs=placed, out_specs=P("aux", "occ", None), check_vma=False
    )
```

time: 543 us -> 142 us (0.26)
  the two profiles are of different devices: /device:TPU:33 before, /device:TPU:1 now
where the time goes in v1:
time: 142 us
  Pallas kernels  135 us (95%)
  local copies, waits for them, and re-layouts  7 us (5%)
    pallas_call x1, Pallas kernels, density(): pl.pallas_call(functools.partial(density_kernel, lax.axis_size('occ')), o...  112 us
    pallas_call x1, Pallas kernels, regroup(): pl.pallas_call(regroup_kernel, out_shape=jax.ShapeDtypeStruct((slabs, row...  14.2 us
    pallas_call x1, Pallas kernels, ungroup(): pl.pallas_call(ungroup_kernel, out_shape=jax.ShapeDtypeStruct(shape, gamm...  8.6 us
    unnamed x9, local copies, waits for them, and re-layouts  7 us

profile of v1, /device:TPU:1, one launch (start us, length us, event | category | flops | bytes accessed | tf_op | source)
XLA Modules:
  0.0 141.6 jit_solution(17924469198467770180)
XLA Ops:
  0.0 1.3 copy.7.mask_ref
  1.3 0.0 copy-start.2
  1.3 1.8 %copy-done.2 = bf16[336,2,2048]{2,1,0:T(2,128)(2,1)S(1)} copy-done((bf16[336,2,2048]{2,1,0:T(2,128)(2,1)S(1)}, bf16[336,2,2048]{2,1,0:T(2,128)(2,1)}, u32[]{:S(2)}) %copy-start.2) | copy-done | bytes 2752536
  3.0 0.0 copy-start.3
  3.1 0.7 copy-done.3
  3.7 14.2 %regroup.1.own_ref = bf16[32,336,128]{2,1,0:T(8,128)(2,1)S(1)} custom-call(s32[32]{0:T(128)S(1)} %copy-done.3, bf16[10752,128]{1,0:T(8,128)(2,1)S(1)} %bitcast.11), custom_call_target="tpu_custom_call" | custom-call | tf_op jit(solution)/shard_map/regroup/pallas_call | solution.py:47
  17.9 0.0 copy-start.1
  17.9 1.5 %copy-done.1 = bf16[32,336,128]{2,1,0:T(8,128)(2,1)} copy-done((bf16[32,336,128]{2,1,0:T(8,128)(2,1)}, bf16[32,336,128]{2,1,0:T(8,128)(2,1)S(1)}, u32[]{:S(2)}) %copy-start.1) | copy-done | bytes 2752536
  19.5 111.8 %density.1.gamma_ref = bf16[32,336,128]{2,1,0:T(8,128)(2,1)} custom-call(s32[32]{0:T(128)} %slab_ref.3, f32[16]{0:T(128)} %occ_ref.1, s32[1,3,32]{2,1,0:T(4,128)} %copy.7.mask_ref, f32[16,128]{1,0:T(8,128)} %bitcast.12, bf16[32,336,128]{2,1,0:T(8,128)(2,1)} %copy-done.1), custom_call_target="tpu_custom_call" | custom-call | tf_op jit(solution)/shard_map/density/pallas_call | solution.py:409
  131.3 0.0 copy-start
  131.3 1.8 %copy-done = bf16[32,336,128]{2,1,0:T(8,128)(2,1)S(1)} copy-done((bf16[32,336,128]{2,1,0:T(8,128)(2,1)S(1)}, bf16[32,336,128]{2,1,0:T(8,128)(2,1)}, u32[]{:S(2)}) %copy-start) | copy-done | bytes 2752536
  133.0 8.6 %ungroup.1 = bf16[10752,128]{1,0:T(8,128)(2,1)} custom-call(bf16[32,336,128]{2,1,0:T(8,128)(2,1)S(1)} %copy-done), custom_call_target="tpu_custom_call" | custom-call | tf_op jit(solution)/shard_map/ungroup/pallas_call | solution.py:81
Async XLA Ops:
  1.3 1.8 %copy-start.2 = (bf16[336,2,2048]{2,1,0:T(2,128)(2,1)S(1)}, bf16[336,2,2048]{2,1,0:T(2,128)(2,1)}, u32[]{:S(2)}) copy-start(bf16[336,2,2048]{2,1,0:T(2,128)(2,1)} %param.5) | copy-start | bytes 8257540
  3.0 0.7 copy-start.3
  17.9 1.5 %copy-start.1 = (bf16[32,336,128]{2,1,0:T(8,128)(2,1)}, bf16[32,336,128]{2,1,0:T(8,128)(2,1)S(1)}, u32[]{:S(2)}) copy-start(bf16[32,336,128]{2,1,0:T(8,128)(2,1)S(1)} %regroup.1.own_ref) | copy-start | bytes 8257540
  131.3 1.8 %copy-start = (bf16[32,336,128]{2,1,0:T(8,128)(2,1)S(1)}, bf16[32,336,128]{2,1,0:T(8,128)(2,1)}, u32[]{:S(2)}) copy-start(bf16[32,336,128]{2,1,0:T(8,128)(2,1)} %density.1.gamma_ref) | copy-start | bytes 8257540

commit v2 on v1

v2 whole, which is shorter than its diff:
```python
import functools

import jax
import jax.numpy as jnp
from jax import lax
from jax.experimental import pallas as pl
from jax.experimental.pallas import tpu as pltpu
from jax.sharding import PartitionSpec as P

SLAB = 64
LANES = 128
X, ZH, CORES = 4, 4, 2
HALF = 16
CHUNK = 4
PIECE = 2
AHEAD = 3
STEP = 16
PART = jnp.bfloat16
MESH = pl.DeviceIdType.MESH
VMEM = pltpu.VMEM


def low_half(shape):
    return lax.broadcasted_iota(jnp.int32, shape, len(shape) - 1) < SLAB


def regroup_kernel(slab_ref, raw_ref, out_ref, wide):
    rows = out_ref.shape[1]

    @pl.loop(0, rows // STEP)
    def _(n):
        at = pl.multiple_of(n * STEP * 32, STEP * 32)
        block = raw_ref[pl.ds(at, STEP * 32), :].astype(jnp.float32)
        wide[:, pl.ds(pl.multiple_of(n * STEP, STEP), STEP), :] = jnp.swapaxes(
            block.reshape(STEP, 32, LANES), 0, 1
        )

    @pl.loop(0, out_ref.shape[0])
    def _(k):
        slab = slab_ref[k]
        odd = slab % 2
        kept = wide[slab]
        moved = pltpu.roll(wide[slab + 1 - 2 * odd], SLAB, 1)
        lane = lax.broadcasted_iota(jnp.int32, kept.shape, 1)
        out_ref[k] = jnp.where(lane // SLAB == odd, kept, moved).astype(out_ref.dtype)


def regroup(raw, slab_owner, rows, slabs):
    return pl.pallas_call(
        regroup_kernel,
        out_shape=jax.ShapeDtypeStruct((slabs, rows, LANES), raw.dtype),
        in_specs=[pl.BlockSpec(memory_space=pltpu.SMEM), pl.BlockSpec(memory_space=VMEM)],
        out_specs=pl.BlockSpec(memory_space=VMEM),
        scratch_shapes=[VMEM((slabs, rows, LANES), jnp.float32)],
        compiler_params=pltpu.CompilerParams(vmem_limit_bytes=24 << 20),
        name="regroup",
    )(slab_owner, raw)


def ungroup_kernel(gamma_ref, raw_ref):
    slabs, rows, _ = gamma_ref.shape

    @pl.loop(0, rows // STEP)
    def _(n):
        at = pl.ds(pl.multiple_of(n * STEP, STEP), STEP)
        block = gamma_ref[:, at, :].astype(jnp.float32).reshape(slabs // 2, 2, STEP, LANES)
        even, odd = block[:, 0], block[:, 1]
        left = low_half(even.shape)
        moved = pltpu.roll(jnp.where(left, odd, even), SLAB, 2)
        pairs = jnp.stack([jnp.where(left, even, moved), jnp.where(left, moved, odd)], axis=1)
        lines = jnp.swapaxes(pairs.reshape(slabs, STEP, LANES), 0, 1)
        to = pl.ds(pl.multiple_of(n * STEP * 32, STEP * 32), STEP * 32)
        raw_ref[to, :] = lines.reshape(STEP * 32, LANES).astype(raw_ref.dtype)


def ungroup(gamma):
    slabs, rows, _ = gamma.shape
    return pl.pallas_call(
        ungroup_kernel,
        out_shape=jax.ShapeDtypeStruct((slabs * rows, LANES), gamma.dtype),
        in_specs=[pl.BlockSpec(memory_space=VMEM)],
        out_specs=pl.BlockSpec(memory_space=VMEM),
        compiler_params=pltpu.CompilerParams(vmem_limit_bytes=24 << 20),
        name="ungroup",
    )(gamma)


def dot(a, b, ca, cb):
    return lax.dot_general(a, b, (((ca,), (cb,)), ((), ())), preferred_element_type=jnp.float32)


def density_kernel(
    occ_count,
    slab_ref, occ_ref, mask_ref, vir_ref, own_ref,
    out_ref,
    panel, near, part, part_wide, part_in, total, unit_out, unit_in, low_in, amp, gamma_out,
    copy_sem, core_send, core_recv, halo_send, halo_recv, x_send, x_recv,
    z_send, z_recv, low_send, low_recv, za_send, za_recv, up_send, up_recv, zl_send, zl_recv,
    xa_send, xa_recv, out_send, out_recv,
):
    o = lax.axis_index("occ")
    aux = lax.axis_index("aux")
    core = aux % CORES
    zh = (aux // CORES) % ZH
    x = aux // (CORES * ZH)
    other = 1 - core

    def device(occ, x_at, z_at, core_at):
        return (occ, (x_at * ZH + z_at) * CORES + core_at)

    below = lax.rem(o + occ_count - 1, occ_count)
    above = lax.rem(o + 1, occ_count)
    x_peers = [lax.rem(x + d, X) for d in range(X)]
    z_peers = [lax.rem(zh + d, ZH) for d in range(ZH)]

    def remote(src, dst, send, recv, to):
        return pltpu.make_async_remote_copy(
            src_ref=src, dst_ref=dst, send_sem=send, recv_sem=recv, device_id=to,
            device_id_type=MESH,
        )

    def arrived(landed, recv, send):
        remote(landed, landed, send, recv, device(above, x, zh, core)).wait_recv()

    partners = [device(o, x, zh, other)]
    partners += [device(b, x, zh, c) for b in (below, above) for c in (0, 1)]
    partners += [device(o, x_peers[d], zh, core) for d in range(1, X)]
    partners += [device(o, x, z_peers[d], core) for d in range(1, ZH)]
    barrier = pltpu.get_barrier_semaphore()
    for partner in partners:
        pl.semaphore_signal(barrier, inc=1, device_id=partner, device_id_type=MESH)
    pl.semaphore_wait(barrier, len(partners))

    chunks = HALF // CHUNK

    def slabs_of(core_at, j):
        return own_ref.at[pl.ds(core_at * HALF + j * CHUNK, CHUNK)]

    def core_copy(j):
        return remote(
            slabs_of(other, j), panel.at[core, pl.ds(j * CHUNK, CHUNK)],
            core_send.at[j], core_recv.at[j], device(o, x, zh, other),
        )

    pieces = HALF // PIECE

    def halo_copy(n, core_at):
        phase, j = divmod(n, pieces)
        way = core if phase == 0 else other
        to = jnp.where(way == 0, below, above)
        return remote(
            own_ref.at[pl.ds(core_at * HALF + j * PIECE, PIECE)],
            near.at[way, core, pl.ds(j * PIECE, PIECE)],
            halo_send.at[n, core_at], halo_recv.at[n, way], device(to, x, zh, core_at),
        )

    def halo_start(n):
        for core_at in (0, 1):
            halo_copy(n, core_at).start()

    def halo_wait_send(n):
        for core_at in (0, 1):
            halo_copy(n, core_at).wait_send()

    def halo_wait_recv(n):
        phase, j = divmod(n, pieces)
        for way in (0, 1):
            source_core = way if phase == 0 else 1 - way
            arrived(near.at[way, source_core, pl.ds(j * PIECE, PIECE)],
                    halo_recv.at[n, way], halo_send.at[n, 0])

    def part_copy(g, d):
        to = x_peers[d]
        return remote(part.at[g, to], part_in.at[g, d], x_send.at[g, d], x_recv.at[g, d],
                      device(o, to, zh, core))

    def coulomb(g, half):
        @pl.loop(half * PIECE, half * PIECE + PIECE)
        def _(s):
            q = g * CHUNK + s
            first, second = panel[0, q], panel[1, q]
            sums = (
                dot(first, first, 0, 0) + dot(second, second, 0, 0),
                dot(first, near[0, 0, q], 0, 0),
                dot(near[1, 1, q], second, 0, 0),
            )
            for m in range(3):
                part_wide[g, s, m] = sums[m]
                part[g, s, m] = sums[m].astype(PART)

        for d in range(1, X):

            @pl.when(x_peers[d] // PIECE == half)
            def _(d=d):
                part_copy(g, d).start()

    def unit_copy(g, d):
        to = z_peers[d]
        return remote(unit_out.at[g, to], unit_in.at[g, d], z_send.at[g, d], z_recv.at[g, d],
                      device(o, x, to, core))

    def unit_start(g, m):
        for d in range(1, ZH):

            @pl.when(z_peers[d] // 2 == m)
            def _(d=d):
                unit_copy(g, d).start()

    def low_copy(g):
        return remote(unit_out.at[g, pl.ds(4, 2)], low_in.at[g], low_send.at[g], low_recv.at[g],
                      device(below, x, zh, core))

    def add_over_x(g):
        for d in range(1, X):
            part_copy(g, d).wait_recv()
        for m in (2, 0, 1):
            value = part_wide[g, x, m]
            for d in range(1, X):
                value = value + part_in[g, d, m].astype(jnp.float32)
            for i in range(2):
                half = value[i * SLAB : (i + 1) * SLAB]
                if m < 2:
                    total[g, 2 * m + i] = half
                if m != 1:
                    unit_out[g, 2 * m + i] = half.astype(PART)
            if m == 2:
                low_copy(g).start()
        unit_start(g, 0)

    def add_low(g):
        low_copy(g).wait_recv()
        for i in range(2):
            value = total[g, 2 + i] + low_in[g, i].astype(jnp.float32)
            total[g, 2 + i] = value
            unit_out[g, 2 + i] = value.astype(PART)
        unit_start(g, 1)

    def amp_copy(g, d):
        mine = amp.at[g * CHUNK + x, zh]
        return remote(mine, mine, za_send.at[g, d], za_recv.at[g, d], device(o, x, z_peers[d], core))

    def amp_up_copy(g):
        q = g * CHUNK + x
        return remote(amp.at[q, zh], amp.at[q, zh + 2], up_send.at[g], up_recv.at[g],
                      device(above, x, zh, core))

    def amp_low_copy(g, d):
        mine = amp.at[g * CHUNK + x, zh + 2]
        return remote(mine, mine, zl_send.at[g, d], zl_recv.at[g, d], device(o, x, z_peers[d], core))

    def amplitude(g):
        for d in range(1, ZH):
            unit_copy(g, d).wait_recv()
        value = total[g, zh]
        for d in range(1, ZH):
            value = value + unit_in[g, d].astype(jnp.float32)
        turned = jnp.concatenate([value, value], axis=0).T
        left = low_half(value.shape)
        swapped = jnp.where(left, turned[:SLAB], turned[SLAB:])
        slab = slab_ref[core * HALF + g * CHUNK + x]
        line = vir_ref[pl.ds(slab // 2, 1), :]
        take = low_half(line.shape) == ((slab % 2) == 0)
        line = jnp.where(take, line, pltpu.roll(line, SLAB, 1))
        eps_b = jnp.broadcast_to(line, (LANES, LANES))
        block = jnp.where(zh < 2, o, above)
        eps_i = occ_ref[2 * o + zh % 2]
        eps_j = jnp.where(left, occ_ref[2 * block], occ_ref[2 * block + 1])
        denominator = eps_b.T[:SLAB] + eps_b[:SLAB] - eps_i - eps_j
        weight = mask_ref[0, 1 + zh // 2, slab].astype(jnp.float32)
        amp[g * CHUNK + x, zh] = (
            (2.0 * value - swapped) / denominator * weight
        ).astype(amp.dtype)

        @pl.when(zh >= 2)
        def _():
            amp_up_copy(g).start()

        for d in range(1, ZH):
            amp_copy(g, d).start()

    def pass_low(g):
        @pl.when(zh >= 2)
        def _():
            amp_up_copy(g).wait_recv()
            for d in range(1, ZH):
                amp_low_copy(g, d).start()

    def panel_copy(g, d):
        mine = amp.at[g * CHUNK + x]
        return remote(mine, mine, xa_send.at[g, d], xa_recv.at[g, d],
                      device(o, x_peers[d], zh, core))

    def gather_over_x(g):
        q = g * CHUNK + x
        for d in range(1, ZH):
            arrived(amp.at[q, z_peers[ZH - d]], za_recv.at[g, d], za_send.at[g, d])

            @pl.when(z_peers[ZH - d] >= 2)
            def _(d=d):
                arrived(amp.at[q, z_peers[ZH - d] + 2], zl_recv.at[g, d], zl_send.at[g, d])

        for d in range(1, X):
            panel_copy(g, d).start()

    def gamma_copy(j):
        return remote(
            gamma_out.at[pl.ds(j * PIECE, PIECE)],
            out_ref.at[pl.ds(core * HALF + j * PIECE, PIECE)],
            out_send.at[j], out_recv.at[j], device(o, x, zh, other),
        )

    def amps_here(g):
        for d in range(1, X):
            arrived(amp.at[g * CHUNK + x_peers[X - d]], xa_recv.at[g, d], xa_send.at[g, d])

    def density(j):
        @pl.loop(0, PIECE)
        def _(s):
            q = j * PIECE + s
            own, up, low = (
                amp[q, 2 * m : 2 * m + 2].reshape(LANES, LANES) for m in range(3)
            )

            def rows(at):
                value = dot(panel[at, q], own, 1, 1) + dot(near[0, at, q], up, 1, 1)
                return (value + dot(near[1, at, q], low, 1, 0)).astype(out_ref.dtype)

            gamma_out[q] = rows(other)
            out_ref[core * HALF + q] = rows(core)

        gamma_copy(j).start()

    local = pltpu.make_async_copy(
        own_ref.at[pl.ds(core * HALF, HALF)], panel.at[core], copy_sem
    )
    for n in range(AHEAD):
        halo_start(n)
        if n == 0:
            local.start()
            core_copy(0).start()
    for j in range(1, chunks):
        core_copy(j).start()
    local.wait()

    schedule = {n: [] for n in range(2 * pieces + 1)}
    for g in range(chunks):
        start = 2 * g
        last = g == chunks - 1
        schedule[start + 3].append((add_over_x, g))
        schedule[start + 4].append((add_low, g))
        schedule[start + (5 if last else 6)].append((amplitude, g))
        schedule[start + (6 if last else 7)].append((pass_low, g))
        schedule[start + 8].append((gather_over_x, g))
        schedule[start + 10].append((amps_here, g))
        schedule[start + 10].append((density, 2 * g))
        schedule[min(start + 11, 2 * pieces)].append((density, 2 * g + 1))
    for n in range(2 * pieces + 1):
        if n < 2 * pieces:
            if n < pieces and n % 2 == 0:
                core_copy(n // 2).wait_recv()
            halo_wait_recv(n)
            halo_wait_send(n)
            if n + AHEAD < 2 * pieces:
                halo_start(n + AHEAD)
            if n < pieces:
                coulomb(n // 2, n % 2)
        for stage, at in schedule[n]:
            stage(at)

    for j in range(pieces):
        gamma_copy(j).wait_send()
    for j in range(chunks):
        core_copy(j).wait_send()
        low_copy(j).wait_send()
        for d in range(1, X):
            part_copy(j, d).wait_send()
            panel_copy(j, d).wait_send()
        for d in range(1, ZH):
            unit_copy(j, d).wait_send()
            amp_copy(j, d).wait_send()

    @pl.when(zh >= 2)
    def _():
        for j in range(chunks):
            amp_up_copy(j).wait_send()
            for d in range(1, ZH):
                amp_low_copy(j, d).wait_send()

    for j in range(pieces):
        arrived(out_ref.at[pl.ds(other * HALF + j * PIECE, PIECE)], out_recv.at[j], out_send.at[j])


def density(grouped, slab_owner, occ_energy, pair_mask, vir_energy):
    slabs, rows, _ = grouped.shape
    dma = pltpu.SemaphoreType.DMA
    bf16, f32 = jnp.bfloat16, jnp.float32
    smem, vmem = pl.BlockSpec(memory_space=pltpu.SMEM), pl.BlockSpec(memory_space=VMEM)
    chunks, pieces = HALF // CHUNK, HALF // PIECE
    return pl.pallas_call(
        functools.partial(density_kernel, lax.axis_size("occ")),
        out_shape=jax.ShapeDtypeStruct(grouped.shape, bf16),
        in_specs=[smem, smem, smem, vmem, vmem],
        out_specs=vmem,
        scratch_shapes=[
            VMEM((2, HALF, rows, LANES), bf16),
            VMEM((2, 2, HALF, rows, LANES), bf16),
            VMEM((chunks, X, 3, LANES, LANES), PART),
            VMEM((chunks, X, 3, LANES, LANES), f32),
            VMEM((chunks, X, 3, LANES, LANES), PART),
            VMEM((chunks, ZH, SLAB, LANES), f32),
            VMEM((chunks, 6, SLAB, LANES), PART),
            VMEM((chunks, ZH, SLAB, LANES), PART),
            VMEM((chunks, 2, SLAB, LANES), PART),
            VMEM((HALF, 6, SLAB, LANES), bf16),
            VMEM((HALF, rows, LANES), bf16),
            dma, dma((chunks,)), dma((chunks,)), dma((2 * pieces, 2)), dma((2 * pieces, 2)),
            dma((chunks, X)), dma((chunks, X)),
            dma((chunks, ZH)), dma((chunks, ZH)), dma((chunks,)), dma((chunks,)),
            dma((chunks, ZH)), dma((chunks, ZH)), dma((chunks,)), dma((chunks,)),
            dma((chunks, ZH)), dma((chunks, ZH)),
            dma((chunks, X)), dma((chunks, X)), dma((pieces,)), dma((pieces,)),
        ],
        compiler_params=pltpu.CompilerParams(
            collective_id=0, has_side_effects=True, vmem_limit_bytes=36 << 20
        ),
        name="density",
    )(slab_owner, occ_energy, pair_mask, vir_energy, grouped)


def on_device(b_factors, occ_energy, vir_energy, slab_owner, pair_mask):
    aux_rows, occ_rows, virtuals = b_factors.shape
    tiles = virtuals // LANES
    raw = b_factors.reshape(aux_rows, occ_rows, tiles, LANES)
    raw = jnp.swapaxes(raw, 1, 2).reshape(aux_rows * tiles * occ_rows, LANES)
    grouped = regroup(raw, slab_owner, aux_rows, virtuals // SLAB)
    gamma = density(
        grouped, slab_owner, occ_energy, pair_mask, vir_energy.reshape(tiles, LANES)
    )
    raw = ungroup(gamma).reshape(aux_rows, tiles, occ_rows, LANES)
    return jnp.swapaxes(raw, 1, 2).reshape(aux_rows, occ_rows, virtuals)


def solution(mesh):
    placed = (P("aux", "occ", None), P(), P(), P(), P("occ", None, None))
    return jax.shard_map(
        on_device, mesh=mesh, in_specs=placed, out_specs=P("aux", "occ", None), check_vma=False
    )
```

time: 142 us -> 119 us (0.84)
  Pallas kernels: 135 us -> 116 us
  local copies, waits for them, and re-layouts: 7 us -> 3.12 us
    pallas_call x1, Pallas kernels: 14.2 us -> 4.92 us  [regroup(): pl.pallas_call(regroup_kernel, out_shape=jax.ShapeDtypeStruct((slabs, row...]
    pallas_call x1, Pallas kernels: 112 us -> 106 us  [density(): pl.pallas_call(functools.partial(density_kernel, lax.axis_size('occ')), o...]
    pallas_call x1, Pallas kernels: 8.6 us -> 4.55 us  [ungroup(): pl.pallas_call(ungroup_kernel, out_shape=jax.ShapeDtypeStruct((slabs * ro...]
    unnamed x9 -> x11, local copies, waits for them, and re-layouts: 7 us -> 3.12 us
where the time goes in v2:
time: 119 us
  Pallas kernels  116 us (97%)
  local copies, waits for them, and re-layouts  3.12 us (3%)
    pallas_call x1, Pallas kernels, density(): pl.pallas_call(functools.partial(density_kernel, lax.axis_size('occ')), o...  106 us
    pallas_call x1, Pallas kernels, regroup(): pl.pallas_call(regroup_kernel, out_shape=jax.ShapeDtypeStruct((slabs, row...  4.92 us
    pallas_call x1, Pallas kernels, ungroup(): pl.pallas_call(ungroup_kernel, out_shape=jax.ShapeDtypeStruct((slabs * ro...  4.55 us
    unnamed x11, local copies, waits for them, and re-layouts  3.12 us

profile of v2, /device:TPU:1, one launch (start us, length us, event | category | flops | bytes accessed | tf_op | source)
XLA Modules:
  0.0 118.9 jit_solution(17286938891312178258)
XLA Ops:
  0.0 0.7 copy.7.mask_ref
  0.7 0.0 copy-start
  0.7 1.8 %copy-done = bf16[336,2,2048]{2,1,0:T(2,128)(2,1)S(1)} copy-done((bf16[336,2,2048]{2,1,0:T(2,128)(2,1)S(1)}, bf16[336,2,2048]{2,1,0:T(2,128)(2,1)}, u32[]{:S(2)}) %copy-start) | copy-done | bytes 2752536
  2.5 0.0 copy-start.2
  2.5 0.7 copy-done.2
  3.1 0.0 copy-start.1
  3.1 0.0 copy-start.3
  3.1 0.0 copy-start.4
  3.1 4.9 %regroup.1.own_ref = bf16[32,336,128]{2,1,0:T(8,128)(2,1)S(1)} custom-call(s32[32]{0:T(128)S(1)} %copy-done.2, bf16[10752,128]{1,0:T(8,128)(2,1)S(1)} %bitcast.11), custom_call_target="tpu_custom_call" | custom-call | tf_op jit(solution)/shard_map/regroup/pallas_call | solution.py:49
  8.1 0.0 copy-done.1
  8.1 0.0 copy-done.3
  8.1 0.0 copy-done.4
  8.1 106.2 %density.1.gamma_ref = bf16[32,336,128]{2,1,0:T(8,128)(2,1)S(1)} custom-call(s32[32]{0:T(128)S(1)} %copy-done.3, f32[16]{0:T(128)S(1)} %copy-done.4, s32[1,3,32]{2,1,0:T(4,128)S(1)} %copy.7.mask_ref, f32[16,128]{1,0:T(8,128)S(1)} %bitcast.12, bf16[32,336,128]{2,1,0:T(8,128)(2,1)S(1)} %regroup.1.own_ref), custom_call_target="tpu_custom_call" | custom-call | tf_op jit(solution)/shard_map/density/pallas_call | solution.py:399
  114.3 4.6 %ungroup.1 = bf16[10752,128]{1,0:T(8,128)(2,1)} custom-call(bf16[32,336,128]{2,1,0:T(8,128)(2,1)S(1)} %density.1.gamma_ref), custom_call_target="tpu_custom_call" | custom-call | tf_op jit(solution)/shard_map/ungroup/pallas_call | solution.py:78
Async XLA Ops:
  0.7 1.8 %copy-start = (bf16[336,2,2048]{2,1,0:T(2,128)(2,1)S(1)}, bf16[336,2,2048]{2,1,0:T(2,128)(2,1)}, u32[]{:S(2)}) copy-start(bf16[336,2,2048]{2,1,0:T(2,128)(2,1)} %param.5) | copy-start | bytes 8257540
  2.5 0.7 copy-start.2
  3.1 4.9 %copy-start.1 = (f32[2048]{0:T(1024)S(1)}, f32[2048]{0:T(1024)}, u32[]{:S(2)}) copy-start(f32[2048]{0:T(1024)} %param.7) | copy-start | bytes 24580
  3.1 4.9 %copy-start.3 = (s32[32]{0:T(128)S(1)}, s32[32]{0:T(128)}, u32[]{:S(2)}) copy-start(s32[32]{0:T(128)} %slab_ref.3) | copy-start | bytes 388
  3.1 5.0 %copy-start.4 = (f32[16]{0:T(128)S(1)}, f32[16]{0:T(128)}, u32[]{:S(2)}) copy-start(f32[16]{0:T(128)} %occ_ref.1) | copy-start | bytes 196

commit v3 on v2

--- a/solution.py
+++ b/solution.py
@@ -13,7 +13,7 @@
 HALF = 16
 CHUNK = 4
 PIECE = 2
-AHEAD = 3
+AHEAD = 4
 STEP = 16
 PART = jnp.bfloat16
 MESH = pl.DeviceIdType.MESH
@@ -154,13 +154,16 @@
             halo_send.at[n, core_at], halo_recv.at[n, way], device(to, x, zh, core_at),
         )
 
-    def halo_start(n):
-        for core_at in (0, 1):
-            halo_copy(n, core_at).start()
-
-    def halo_wait_send(n):
-        for core_at in (0, 1):
-            halo_copy(n, core_at).wait_send()
+    halos = [(n, core_at) for n in range(2 * pieces) for core_at in (0, 1)]
+    finished = []
+
+    def advance():
+        at = len(finished)
+        if at < len(halos):
+            halo_copy(*halos[at]).wait_send()
+            finished.append(at)
+            if at + AHEAD < len(halos):
+                halo_copy(*halos[at + AHEAD]).start()
 
     def halo_wait_recv(n):
         phase, j = divmod(n, pieces)
@@ -333,38 +336,36 @@
     local = pltpu.make_async_copy(
         own_ref.at[pl.ds(core * HALF, HALF)], panel.at[core], copy_sem
     )
-    for n in range(AHEAD):
-        halo_start(n)
-        if n == 0:
-            local.start()
-            core_copy(0).start()
+    for at in range(AHEAD):
+        halo_copy(*halos[at]).start()
+    local.start()
+    core_copy(0).start()
     for j in range(1, chunks):
         core_copy(j).start()
     local.wait()
 
+    steps = ((2, 3, 4, 5, 6, 8), (4, 5, 6, 7, 8, 10), (6, 7, 8, 9, 10, 12), (8, 9, 10, 11, 12, 14))
     schedule = {n: [] for n in range(2 * pieces + 1)}
+    for at, stage in enumerate((add_over_x, add_low, amplitude, pass_low, gather_over_x, amps_here)):
+        for g in range(chunks):
+            schedule[steps[g][at]].append((stage, g))
     for g in range(chunks):
-        start = 2 * g
-        last = g == chunks - 1
-        schedule[start + 3].append((add_over_x, g))
-        schedule[start + 4].append((add_low, g))
-        schedule[start + (5 if last else 6)].append((amplitude, g))
-        schedule[start + (6 if last else 7)].append((pass_low, g))
-        schedule[start + 8].append((gather_over_x, g))
-        schedule[start + 10].append((amps_here, g))
-        schedule[start + 10].append((density, 2 * g))
-        schedule[min(start + 11, 2 * pieces)].append((density, 2 * g + 1))
+        for j in range(2):
+            ready = max(steps[g][5], pieces + 2 * g + j)
+            schedule[ready].append((density, 2 * g + j))
     for n in range(2 * pieces + 1):
         if n < 2 * pieces:
             if n < pieces and n % 2 == 0:
                 core_copy(n // 2).wait_recv()
             halo_wait_recv(n)
-            halo_wait_send(n)
-            if n + AHEAD < 2 * pieces:
-                halo_start(n + AHEAD)
+            advance()
             if n < pieces:
                 coulomb(n // 2, n % 2)
-        for stage, at in schedule[n]:
+        stages = list(schedule[n])
+        for stage, at in stages[: len(stages) // 2]:
+            stage(at)
+        advance()
+        for stage, at in stages[len(stages) // 2 :]:
             stage(at)
 
     for j in range(pieces):

time: 119 us -> 109 us (0.916)
  Pallas kernels: 116 us -> 105 us
    pallas_call x1, Pallas kernels: 106 us -> 95.8 us  [density(): pl.pallas_call(functools.partial(density_kernel, lax.axis_size('occ')), o...]
where the time goes in v3:
time: 109 us; the launch traced here: 108 us
  Pallas kernels  105 us (96%)
  local copies, waits for them, and re-layouts  3.12 us (3%)
    pallas_call x1, Pallas kernels, density(): pl.pallas_call(functools.partial(density_kernel, lax.axis_size('occ')), o...  95.8 us
    pallas_call x1, Pallas kernels, regroup(): pl.pallas_call(regroup_kernel, out_shape=jax.ShapeDtypeStruct((slabs, row...  4.92 us
    pallas_call x1, Pallas kernels, ungroup(): pl.pallas_call(ungroup_kernel, out_shape=jax.ShapeDtypeStruct((slabs * ro...  4.55 us
    unnamed x11, local copies, waits for them, and re-layouts  3.12 us

profile of v3, /device:TPU:1, one launch (start us, length us, event | category | flops | bytes accessed | tf_op | source)
XLA Modules:
  0.0 108.4 jit_solution(6772914876899427258)
XLA Ops:
  0.0 0.7 copy.7.mask_ref
  0.7 0.0 copy-start
  0.7 1.8 %copy-done = bf16[336,2,2048]{2,1,0:T(2,128)(2,1)S(1)} copy-done((bf16[336,2,2048]{2,1,0:T(2,128)(2,1)S(1)}, bf16[336,2,2048]{2,1,0:T(2,128)(2,1)}, u32[]{:S(2)}) %copy-start) | copy-done | bytes 2752536
  2.5 0.0 copy-start.2
  2.5 0.7 copy-done.2
  3.1 0.0 copy-start.1
  3.1 0.0 copy-start.3
  3.1 0.0 copy-start.4
  3.1 4.9 %regroup.1.own_ref = bf16[32,336,128]{2,1,0:T(8,128)(2,1)S(1)} custom-call(s32[32]{0:T(128)S(1)} %copy-done.2, bf16[10752,128]{1,0:T(8,128)(2,1)S(1)} %bitcast.11), custom_call_target="tpu_custom_call" | custom-call | tf_op jit(solution)/shard_map/regroup/pallas_call | solution.py:49
  8.1 0.0 copy-done.1
  8.1 0.0 copy-done.3
  8.1 0.0 copy-done.4
  8.1 95.8 %density.1.gamma_ref = bf16[32,336,128]{2,1,0:T(8,128)(2,1)S(1)} custom-call(s32[32]{0:T(128)S(1)} %copy-done.3, f32[16]{0:T(128)S(1)} %copy-done.4, s32[1,3,32]{2,1,0:T(4,128)S(1)} %copy.7.mask_ref, f32[16,128]{1,0:T(8,128)S(1)} %bitcast.12, bf16[32,336,128]{2,1,0:T(8,128)(2,1)S(1)} %regroup.1.own_ref), custom_call_target="tpu_custom_call" | custom-call | tf_op jit(solution)/shard_map/density/pallas_call | solution.py:400
  103.8 4.6 %ungroup.1 = bf16[10752,128]{1,0:T(8,128)(2,1)} custom-call(bf16[32,336,128]{2,1,0:T(8,128)(2,1)S(1)} %density.1.gamma_ref), custom_call_target="tpu_custom_call" | custom-call | tf_op jit(solution)/shard_map/ungroup/pallas_call | solution.py:78
Async XLA Ops:
  0.7 1.8 %copy-start = (bf16[336,2,2048]{2,1,0:T(2,128)(2,1)S(1)}, bf16[336,2,2048]{2,1,0:T(2,128)(2,1)}, u32[]{:S(2)}) copy-start(bf16[336,2,2048]{2,1,0:T(2,128)(2,1)} %param.5) | copy-start | bytes 8257540
  2.5 0.7 copy-start.2
  3.1 4.9 %copy-start.1 = (f32[2048]{0:T(1024)S(1)}, f32[2048]{0:T(1024)}, u32[]{:S(2)}) copy-start(f32[2048]{0:T(1024)} %param.7) | copy-start | bytes 24580
  3.1 4.9 %copy-start.3 = (s32[32]{0:T(128)S(1)}, s32[32]{0:T(128)}, u32[]{:S(2)}) copy-start(s32[32]{0:T(128)} %slab_ref.3) | copy-start | bytes 388
  3.1 5.0 %copy-start.4 = (f32[16]{0:T(128)S(1)}, f32[16]{0:T(128)}, u32[]{:S(2)}) copy-start(f32[16]{0:T(128)} %occ_ref.1) | copy-start | bytes 196

commit v4 on v3

--- a/solution.py
+++ b/solution.py
@@ -24,10 +24,8 @@
     return lax.broadcasted_iota(jnp.int32, shape, len(shape) - 1) < SLAB
 
 
-def regroup_kernel(slab_ref, raw_ref, out_ref, wide):
-    rows = out_ref.shape[1]
-
-    @pl.loop(0, rows // STEP)
+def split_rows(raw_ref, wide):
+    @pl.loop(0, wide.shape[1] // STEP)
     def _(n):
         at = pl.multiple_of(n * STEP * 32, STEP * 32)
         block = raw_ref[pl.ds(at, STEP * 32), :].astype(jnp.float32)
@@ -35,26 +33,13 @@
             block.reshape(STEP, 32, LANES), 0, 1
         )
 
-    @pl.loop(0, out_ref.shape[0])
-    def _(k):
-        slab = slab_ref[k]
-        odd = slab % 2
-        kept = wide[slab]
-        moved = pltpu.roll(wide[slab + 1 - 2 * odd], SLAB, 1)
-        lane = lax.broadcasted_iota(jnp.int32, kept.shape, 1)
-        out_ref[k] = jnp.where(lane // SLAB == odd, kept, moved).astype(out_ref.dtype)
-
-
-def regroup(raw, slab_owner, rows, slabs):
-    return pl.pallas_call(
-        regroup_kernel,
-        out_shape=jax.ShapeDtypeStruct((slabs, rows, LANES), raw.dtype),
-        in_specs=[pl.BlockSpec(memory_space=pltpu.SMEM), pl.BlockSpec(memory_space=VMEM)],
-        out_specs=pl.BlockSpec(memory_space=VMEM),
-        scratch_shapes=[VMEM((slabs, rows, LANES), jnp.float32)],
-        compiler_params=pltpu.CompilerParams(vmem_limit_bytes=24 << 20),
-        name="regroup",
-    )(slab_owner, raw)
+
+def slab_panel(slab, wide):
+    odd = slab % 2
+    kept = wide[slab]
+    moved = pltpu.roll(wide[slab + 1 - 2 * odd], SLAB, 1)
+    lane = lax.broadcasted_iota(jnp.int32, kept.shape, 1)
+    return jnp.where(lane // SLAB == odd, kept, moved).astype(jnp.bfloat16)
 
 
 def ungroup_kernel(gamma_ref, raw_ref):
@@ -91,8 +76,9 @@
 
 def density_kernel(
     occ_count,
-    slab_ref, occ_ref, mask_ref, vir_ref, own_ref,
+    slab_ref, occ_ref, mask_ref, vir_ref, raw_ref,
     out_ref,
+    own_ref, wide,
     panel, near, part, part_wide, part_in, total, unit_out, unit_in, low_in, amp, gamma_out,
     copy_sem, core_send, core_recv, halo_send, halo_recv, x_send, x_recv,
     z_send, z_recv, low_send, low_recv, za_send, za_recv, up_send, up_recv, zl_send, zl_recv,
@@ -129,6 +115,15 @@
     barrier = pltpu.get_barrier_semaphore()
     for partner in partners:
         pl.semaphore_signal(barrier, inc=1, device_id=partner, device_id_type=MESH)
+    split_rows(raw_ref, wide)
+
+    def regroup(first, last):
+        @pl.loop(first, last)
+        def _(q):
+            for k in (q, HALF + q):
+                own_ref[k] = slab_panel(slab_ref[k], wide)
+
+    regroup(0, CHUNK)
     pl.semaphore_wait(barrier, len(partners))
 
     chunks = HALF // CHUNK
@@ -338,8 +333,9 @@
     )
     for at in range(AHEAD):
         halo_copy(*halos[at]).start()
+    core_copy(0).start()
+    regroup(CHUNK, HALF)
     local.start()
-    core_copy(0).start()
     for j in range(1, chunks):
         core_copy(j).start()
     local.wait()
@@ -391,18 +387,20 @@
         arrived(out_ref.at[pl.ds(other * HALF + j * PIECE, PIECE)], out_recv.at[j], out_send.at[j])
 
 
-def density(grouped, slab_owner, occ_energy, pair_mask, vir_energy):
-    slabs, rows, _ = grouped.shape
+def density(raw, rows, slab_owner, occ_energy, pair_mask, vir_energy):
+    slabs = raw.shape[0] // rows
     dma = pltpu.SemaphoreType.DMA
     bf16, f32 = jnp.bfloat16, jnp.float32
     smem, vmem = pl.BlockSpec(memory_space=pltpu.SMEM), pl.BlockSpec(memory_space=VMEM)
     chunks, pieces = HALF // CHUNK, HALF // PIECE
     return pl.pallas_call(
         functools.partial(density_kernel, lax.axis_size("occ")),
-        out_shape=jax.ShapeDtypeStruct(grouped.shape, bf16),
+        out_shape=jax.ShapeDtypeStruct((slabs, rows, LANES), bf16),
         in_specs=[smem, smem, smem, vmem, vmem],
         out_specs=vmem,
         scratch_shapes=[
+            VMEM((slabs, rows, LANES), bf16),
+            VMEM((slabs, rows, LANES), f32),
             VMEM((2, HALF, rows, LANES), bf16),
             VMEM((2, 2, HALF, rows, LANES), bf16),
             VMEM((chunks, X, 3, LANES, LANES), PART),
@@ -425,7 +423,7 @@
             collective_id=0, has_side_effects=True, vmem_limit_bytes=36 << 20
         ),
         name="density",
-    )(slab_owner, occ_energy, pair_mask, vir_energy, grouped)
+    )(slab_owner, occ_energy, pair_mask, vir_energy, raw)
 
 
 def on_device(b_factors, occ_energy, vir_energy, slab_owner, pair_mask):
@@ -433,9 +431,8 @@
     tiles = virtuals // LANES
     raw = b_factors.reshape(aux_rows, occ_rows, tiles, LANES)
     raw = jnp.swapaxes(raw, 1, 2).reshape(aux_rows * tiles * occ_rows, LANES)
-    grouped = regroup(raw, slab_owner, aux_rows, virtuals // SLAB)
     gamma = density(
-        grouped, slab_owner, occ_energy, pair_mask, vir_energy.reshape(tiles, LANES)
+        raw, aux_rows, slab_owner, occ_energy, pair_mask, vir_energy.reshape(tiles, LANES)
     )
     raw = ungroup(gamma).reshape(aux_rows, tiles, occ_rows, LANES)
     return jnp.swapaxes(raw, 1, 2).reshape(aux_rows, occ_rows, virtuals)

time: 109 us -> 105 us (0.963)
  Pallas kernels: 105 us -> 100 us
  local copies, waits for them, and re-layouts: 3.12 us -> 4.46 us
    pallas_call x1 -> x0, Pallas kernels: 4.92 us -> none  [regroup(): pl.pallas_call(regroup_kernel, out_shape=jax.ShapeDtypeStruct((slabs, row...]
    unnamed x11 -> x9, local copies, waits for them, and re-layouts: 3.12 us -> 4.46 us
where the time goes in v4:
time: 105 us
  Pallas kernels  100 us (95%)
  local copies, waits for them, and re-layouts  4.46 us (4%)
    pallas_call x1, Pallas kernels, density(): pl.pallas_call(functools.partial(density_kernel, lax.axis_size('occ')), o...  95.6 us
    pallas_call x1, Pallas kernels, ungroup(): pl.pallas_call(ungroup_kernel, out_shape=jax.ShapeDtypeStruct((slabs * ro...  4.55 us
    unnamed x9, local copies, waits for them, and re-layouts  4.46 us

profile of v4, /device:TPU:1, one launch (start us, length us, event | category | flops | bytes accessed | tf_op | source)
XLA Modules:
  0.0 104.7 jit_solution(6350621759167951435)
XLA Ops:
  0.0 0.7 copy.7.mask_ref
  0.7 0.0 copy-start
  0.7 1.8 %copy-done = bf16[336,2,2048]{2,1,0:T(2,128)(2,1)S(1)} copy-done((bf16[336,2,2048]{2,1,0:T(2,128)(2,1)S(1)}, bf16[336,2,2048]{2,1,0:T(2,128)(2,1)}, u32[]{:S(2)}) %copy-start) | copy-done | bytes 2752536
  2.5 0.0 copy-start.1
  2.5 0.7 copy-done.1
  3.2 0.0 copy-start.2
  3.2 0.7 copy-done.2
  3.8 0.0 copy-start.3
  3.8 0.7 copy-done.3
  4.5 95.6 %density.1.gamma_ref = bf16[32,336,128]{2,1,0:T(8,128)(2,1)S(1)} custom-call(s32[32]{0:T(128)S(1)} %copy-done.2, f32[16]{0:T(128)S(1)} %copy-done.3, s32[1,3,32]{2,1,0:T(4,128)S(1)} %copy.7.mask_ref, f32[16,128]{1,0:T(8,128)S(1)} %bitcast.12, bf16[10752,128]{1,0:T(8,128)(2,1)S(1)} %bitcast.11), custom_call_target="tpu_custom_call" | custom-call | tf_op jit(solution)/shard_map/density/pallas_call | solution.py:396
  100.1 4.6 %ungroup.1 = bf16[10752,128]{1,0:T(8,128)(2,1)} custom-call(bf16[32,336,128]{2,1,0:T(8,128)(2,1)S(1)} %density.1.gamma_ref), custom_call_target="tpu_custom_call" | custom-call | tf_op jit(solution)/shard_map/ungroup/pallas_call | solution.py:63
Async XLA Ops:
  0.7 1.8 %copy-start = (bf16[336,2,2048]{2,1,0:T(2,128)(2,1)S(1)}, bf16[336,2,2048]{2,1,0:T(2,128)(2,1)}, u32[]{:S(2)}) copy-start(bf16[336,2,2048]{2,1,0:T(2,128)(2,1)} %param.5) | copy-start | bytes 8257540
  2.5 0.7 copy-start.1
  3.2 0.7 copy-start.2
  3.8 0.7 copy-start.3

commit v5 on v4

--- a/solution.py
+++ b/solution.py
@@ -42,11 +42,10 @@
     return jnp.where(lane // SLAB == odd, kept, moved).astype(jnp.bfloat16)
 
 
-def ungroup_kernel(gamma_ref, raw_ref):
+def ungroup_kernel(gamma_in, out_ref, gamma_ref, raw_ref, load_sem, sem):
     slabs, rows, _ = gamma_ref.shape
 
-    @pl.loop(0, rows // STEP)
-    def _(n):
+    def lay_out(n):
         at = pl.ds(pl.multiple_of(n * STEP, STEP), STEP)
         block = gamma_ref[:, at, :].astype(jnp.float32).reshape(slabs // 2, 2, STEP, LANES)
         even, odd = block[:, 0], block[:, 1]
@@ -57,15 +56,38 @@
         to = pl.ds(pl.multiple_of(n * STEP * 32, STEP * 32), STEP * 32)
         raw_ref[to, :] = lines.reshape(STEP * 32, LANES).astype(raw_ref.dtype)
 
+    shares = 3
+    share = raw_ref.shape[0] // shares
+    steps = rows // STEP // shares
+    loads, stores = [], []
+    for at in range(shares):
+        part = pl.ds(at * steps * STEP, steps * STEP)
+        loads.append(
+            pltpu.make_async_copy(gamma_in.at[:, part], gamma_ref.at[:, part], load_sem.at[at])
+        )
+        loads[-1].start()
+    for at in range(shares):
+        loads[at].wait()
+        pl.loop(at * steps, (at + 1) * steps)(lay_out)
+        done = pl.ds(at * share, share)
+        stores.append(pltpu.make_async_copy(raw_ref.at[done], out_ref.at[done], sem.at[at]))
+        stores[-1].start()
+    for store in stores:
+        store.wait()
+
 
 def ungroup(gamma):
     slabs, rows, _ = gamma.shape
     return pl.pallas_call(
         ungroup_kernel,
         out_shape=jax.ShapeDtypeStruct((slabs * rows, LANES), gamma.dtype),
-        in_specs=[pl.BlockSpec(memory_space=VMEM)],
-        out_specs=pl.BlockSpec(memory_space=VMEM),
-        compiler_params=pltpu.CompilerParams(vmem_limit_bytes=24 << 20),
+        in_specs=[pl.BlockSpec(memory_space=pltpu.HBM)],
+        out_specs=pl.BlockSpec(memory_space=pltpu.HBM),
+        scratch_shapes=[
+            VMEM(gamma.shape, gamma.dtype), VMEM((slabs * rows, LANES), gamma.dtype),
+            pltpu.SemaphoreType.DMA((3,)), pltpu.SemaphoreType.DMA((3,)),
+        ],
+        compiler_params=pltpu.CompilerParams(vmem_limit_bytes=57 << 20),
         name="ungroup",
     )(gamma)
 
@@ -76,13 +98,14 @@
 
 def density_kernel(
     occ_count,
-    slab_ref, occ_ref, mask_ref, vir_ref, raw_ref,
+    slab_in, occ_in, mask_in, vir_in, raw_in,
     out_ref,
+    slab_ref, occ_ref, mask_ref, vir_ref, raw_ref, load_sem,
     own_ref, wide,
-    panel, near, part, part_wide, part_in, total, unit_out, unit_in, low_in, amp, gamma_out,
+    panel, near, part, part_wide, part_in, total, unit_out, unit_in, low_in, amp, gamma_out, gamma_own,
     copy_sem, core_send, core_recv, halo_send, halo_recv, x_send, x_recv,
     z_send, z_recv, low_send, low_recv, za_send, za_recv, up_send, up_recv, zl_send, zl_recv,
-    xa_send, xa_recv, out_send, out_recv,
+    xa_send, xa_recv, out_send, out_recv, store_sem,
 ):
     o = lax.axis_index("occ")
     aux = lax.axis_index("aux")
@@ -112,9 +135,20 @@
     partners += [device(b, x, zh, c) for b in (below, above) for c in (0, 1)]
     partners += [device(o, x_peers[d], zh, core) for d in range(1, X)]
     partners += [device(o, x, z_peers[d], core) for d in range(1, ZH)]
+    loads = [
+        pltpu.make_async_copy(source, landing, load_sem.at[n])
+        for n, (source, landing) in enumerate((
+            (raw_in, raw_ref), (slab_in, slab_ref), (occ_in, occ_ref), (mask_in, mask_ref),
+            (vir_in, vir_ref),
+        ))
+    ]
+    for load in loads:
+        load.start()
     barrier = pltpu.get_barrier_semaphore()
     for partner in partners:
         pl.semaphore_signal(barrier, inc=1, device_id=partner, device_id_type=MESH)
+    for load in loads:
+        load.wait()
     split_rows(raw_ref, wide)
 
     def regroup(first, last):
@@ -264,7 +298,7 @@
         eps_i = occ_ref[2 * o + zh % 2]
         eps_j = jnp.where(left, occ_ref[2 * block], occ_ref[2 * block + 1])
         denominator = eps_b.T[:SLAB] + eps_b[:SLAB] - eps_i - eps_j
-        weight = mask_ref[0, 1 + zh // 2, slab].astype(jnp.float32)
+        weight = mask_ref[1 + zh // 2, 0, slab].astype(jnp.float32)
         amp[g * CHUNK + x, zh] = (
             (2.0 * value - swapped) / denominator * weight
         ).astype(amp.dtype)
@@ -305,6 +339,12 @@
             gamma_out.at[pl.ds(j * PIECE, PIECE)],
             out_ref.at[pl.ds(core * HALF + j * PIECE, PIECE)],
             out_send.at[j], out_recv.at[j], device(o, x, zh, other),
+        )
+
+    def store(j):
+        return pltpu.make_async_copy(
+            gamma_own.at[pl.ds(j * PIECE, PIECE)],
+            out_ref.at[pl.ds(core * HALF + j * PIECE, PIECE)], store_sem.at[j],
         )
 
     def amps_here(g):
@@ -324,9 +364,10 @@
                 return (value + dot(near[1, at, q], low, 1, 0)).astype(out_ref.dtype)
 
             gamma_out[q] = rows(other)
-            out_ref[core * HALF + q] = rows(core)
+            gamma_own[q] = rows(core)
 
         gamma_copy(j).start()
+        store(j).start()
 
     local = pltpu.make_async_copy(
         own_ref.at[pl.ds(core * HALF, HALF)], panel.at[core], copy_sem
@@ -366,6 +407,7 @@
 
     for j in range(pieces):
         gamma_copy(j).wait_send()
+        store(j).wait()
     for j in range(chunks):
         core_copy(j).wait_send()
         low_copy(j).wait_send()
@@ -391,14 +433,21 @@
     slabs = raw.shape[0] // rows
     dma = pltpu.SemaphoreType.DMA
     bf16, f32 = jnp.bfloat16, jnp.float32
-    smem, vmem = pl.BlockSpec(memory_space=pltpu.SMEM), pl.BlockSpec(memory_space=VMEM)
+    hbm = pl.BlockSpec(memory_space=pltpu.HBM)
+    smem = pltpu.SMEM
     chunks, pieces = HALF // CHUNK, HALF // PIECE
     return pl.pallas_call(
         functools.partial(density_kernel, lax.axis_size("occ")),
         out_shape=jax.ShapeDtypeStruct((slabs, rows, LANES), bf16),
-        in_specs=[smem, smem, smem, vmem, vmem],
-        out_specs=vmem,
+        in_specs=[hbm] * 5,
+        out_specs=hbm,
         scratch_shapes=[
+            smem(slab_owner.shape, slab_owner.dtype),
+            smem(occ_energy.shape, f32),
+            smem(pair_mask.shape, pair_mask.dtype),
+            VMEM(vir_energy.shape, f32),
+            VMEM(raw.shape, bf16),
+            dma((5,)),
             VMEM((slabs, rows, LANES), bf16),
             VMEM((slabs, rows, LANES), f32),
             VMEM((2, HALF, rows, LANES), bf16),
@@ -412,15 +461,16 @@
             VMEM((chunks, 2, SLAB, LANES), PART),
             VMEM((HALF, 6, SLAB, LANES), bf16),
             VMEM((HALF, rows, LANES), bf16),
+            VMEM((HALF, rows, LANES), bf16),
             dma, dma((chunks,)), dma((chunks,)), dma((2 * pieces, 2)), dma((2 * pieces, 2)),
             dma((chunks, X)), dma((chunks, X)),
             dma((chunks, ZH)), dma((chunks, ZH)), dma((chunks,)), dma((chunks,)),
             dma((chunks, ZH)), dma((chunks, ZH)), dma((chunks,)), dma((chunks,)),
             dma((chunks, ZH)), dma((chunks, ZH)),
-            dma((chunks, X)), dma((chunks, X)), dma((pieces,)), dma((pieces,)),
+            dma((chunks, X)), dma((chunks, X)), dma((pieces,)), dma((pieces,)), dma((pieces,)),
         ],
         compiler_params=pltpu.CompilerParams(
-            collective_id=0, has_side_effects=True, vmem_limit_bytes=36 << 20
+            collective_id=0, has_side_effects=True, vmem_limit_bytes=57 << 20
         ),
         name="density",
     )(slab_owner, occ_energy, pair_mask, vir_energy, raw)
@@ -432,7 +482,8 @@
     raw = b_factors.reshape(aux_rows, occ_rows, tiles, LANES)
     raw = jnp.swapaxes(raw, 1, 2).reshape(aux_rows * tiles * occ_rows, LANES)
     gamma = density(
-        raw, aux_rows, slab_owner, occ_energy, pair_mask, vir_energy.reshape(tiles, LANES)
+        raw, aux_rows, slab_owner, occ_energy, jnp.swapaxes(pair_mask, 0, 1),
+        vir_energy.reshape(tiles, LANES),
     )
     raw = ungroup(gamma).reshape(aux_rows, tiles, occ_rows, LANES)
     return jnp.swapaxes(raw, 1, 2).reshape(aux_rows, occ_rows, virtuals)

time: 105 us -> 100 us (0.952)
  local copies, waits for them, and re-layouts: 4.46 us -> 0 us
    unnamed x9 -> x0, local copies, waits for them, and re-layouts: 4.46 us -> none
where the time goes in v5:
time: 100 us
  Pallas kernels  100 us (100%)
    pallas_call x1, Pallas kernels, density(): pl.pallas_call(functools.partial(density_kernel, lax.axis_size('occ')), o...  95.4 us
    pallas_call x1, Pallas kernels, ungroup(): pl.pallas_call(ungroup_kernel, out_shape=jax.ShapeDtypeStruct((slabs * ro...  4.98 us

profile of v5, /device:TPU:1, one launch (start us, length us, event | category | flops | bytes accessed | tf_op | source)
XLA Modules:
  0.0 100.4 jit_solution(15513937723960061736)
XLA Ops:
  0.0 95.4 %density.1.gamma_in = bf16[32,336,128]{2,1,0:T(8,128)(2,1)} custom-call(s32[32]{0:T(128)} %slab_in.1, f32[16]{0:T(128)} %occ_in.1, s32[3,1,32]{2,1,0:T(1,128)} %bitcast.14, f32[16,128]{1,0:T(8,128)} %bitcast.13, bf16[10752,128]{1,0:T(8,128)(2,1)} %bitcast.12), custom_call_target="tpu_custom_call" | custom-call | tf_op jit(solution)/shard_map/density/pallas_call | solution.py:439
  95.4 5.0 %ungroup.1 = bf16[10752,128]{1,0:T(8,128)(2,1)} custom-call(bf16[32,336,128]{2,1,0:T(8,128)(2,1)} %density.1.gamma_in), custom_call_target="tpu_custom_call" | custom-call | tf_op jit(solution)/shard_map/ungroup/pallas_call | solution.py:81

commit v6 on v5

--- a/solution.py
+++ b/solution.py
@@ -13,6 +13,7 @@
 HALF = 16
 CHUNK = 4
 PIECE = 2
+FAR_FIRST = (2, 1, 3)
 AHEAD = 4
 STEP = 16
 PART = jnp.bfloat16
@@ -220,7 +221,7 @@
                 part_wide[g, s, m] = sums[m]
                 part[g, s, m] = sums[m].astype(PART)
 
-        for d in range(1, X):
+        for d in FAR_FIRST:
 
             @pl.when(x_peers[d] // PIECE == half)
             def _(d=d):
@@ -232,7 +233,7 @@
                       device(o, x, to, core))
 
     def unit_start(g, m):
-        for d in range(1, ZH):
+        for d in FAR_FIRST:
 
             @pl.when(z_peers[d] // 2 == m)
             def _(d=d):
@@ -307,14 +308,14 @@
         def _():
             amp_up_copy(g).start()
 
-        for d in range(1, ZH):
+        for d in FAR_FIRST:
             amp_copy(g, d).start()
 
     def pass_low(g):
         @pl.when(zh >= 2)
         def _():
             amp_up_copy(g).wait_recv()
-            for d in range(1, ZH):
+            for d in FAR_FIRST:
                 amp_low_copy(g, d).start()
 
     def panel_copy(g, d):
@@ -331,7 +332,7 @@
             def _(d=d):
                 arrived(amp.at[q, z_peers[ZH - d] + 2], zl_recv.at[g, d], zl_send.at[g, d])
 
-        for d in range(1, X):
+        for d in FAR_FIRST:
             panel_copy(g, d).start()
 
     def gamma_copy(j):

time: 100 us -> 100 us (level)
  no operation moved by 1% of the time
where the time goes in v6:
time: 100 us
  Pallas kernels  100 us (100%)
    pallas_call x1, Pallas kernels, density(): pl.pallas_call(functools.partial(density_kernel, lax.axis_size('occ')), o...  95.3 us
    pallas_call x1, Pallas kernels, ungroup(): pl.pallas_call(ungroup_kernel, out_shape=jax.ShapeDtypeStruct((slabs * ro...  4.98 us

profile of v6, /device:TPU:1, one launch (start us, length us, event | category | flops | bytes accessed | tf_op | source)
XLA Modules:
  0.0 100.3 jit_solution(18117270467349009363)
XLA Ops:
  0.0 95.3 %density.1.gamma_in = bf16[32,336,128]{2,1,0:T(8,128)(2,1)} custom-call(s32[32]{0:T(128)} %slab_in.1, f32[16]{0:T(128)} %occ_in.1, s32[3,1,32]{2,1,0:T(1,128)} %bitcast.14, f32[16,128]{1,0:T(8,128)} %bitcast.13, bf16[10752,128]{1,0:T(8,128)(2,1)} %bitcast.12), custom_call_target="tpu_custom_call" | custom-call | tf_op jit(solution)/shard_map/density/pallas_call | solution.py:440
  95.3 5.0 %ungroup.1 = bf16[10752,128]{1,0:T(8,128)(2,1)} custom-call(bf16[32,336,128]{2,1,0:T(8,128)(2,1)} %density.1.gamma_in), custom_call_target="tpu_custom_call" | custom-call | tf_op jit(solution)/shard_map/ungroup/pallas_call | solution.py:82
